TPU v7x, 256 devices: a whole 4x4x8 slice. The times are simulated.
256 devices in a mesh: layer: 8 (over z), plane: 32 (over y, x, core).
Axes of the slice: x: 4, y: 4, z: 8, core: 2. Of those that a mesh axis runs over, the one named last changes fastest.
Arguments:
- leaf_rhs: bfloat16 [2048, 128, 512], P(('layer', 'plane')), may hold values from -6 to 6
- leaf_inverse: bfloat16 [2048, 128, 128], P(('layer', 'plane')), may hold values from -0.5 to 0.5
- leaf_couple: bfloat16 [2048, 3, 1024, 128], P(('layer', 'plane')), may hold values from -0.09375 to 0.09375
- couple_mask: int32 [2048, 3], P(('layer', 'plane')), may hold values 0 or 1
- leaf_diag: float32 [2048, 128], P(('layer', 'plane')), may hold values from 0.5 to 2
- sep_rhs: bfloat16 [7, 1024, 512], P(None, 'plane'), may hold values from -6 to 6
- sep_inverse: bfloat16 [7, 1024, 1024], P(None, 'plane'), may hold values from -0.1875 to 0.1875
- sep_couple: bfloat16 [7, 2, 1024, 1024], P(None, None, 'plane'), may hold values from -0.125 to 0.125
- sep_diag: float32 [7, 1024], P(None, 'plane'), may hold values from 0.5 to 2
Outputs:
- leaf_solution: bfloat16 [2048, 128, 512], P(('layer', 'plane'))
- sep_solution: bfloat16 [8, 3, 1024, 512], P('layer', None, 'plane')
All inputs are finite; a program needn't handle non-finite values. No bound on the sum of `couple_mask` on one device may be relied on, other than what follows from the above.
Results may differ from a plain program's by a relative error of at most 0.02.
Values may be sent and summed in bfloat16 or wider, within the bound.
A program may use at most 128 MiB of HBM per device.

v0:
```python
import jax
import jax.numpy as jnp
from jax import lax
from jax.sharding import PartitionSpec as P


def from_partner(value, axis, stride):
    mask = 2**stride
    pairs = [(source, source ^ mask) for source in range(lax.axis_size(axis))]
    return lax.ppermute(value, axis, pairs)


def lower_unit(block, first_row):
    row_count = block.shape[-2]
    col_count = block.shape[-1]
    row_ids = first_row + lax.broadcasted_iota(jnp.int32, (row_count, col_count), 0)
    col_ids = lax.broadcasted_iota(jnp.int32, (row_count, col_count), 1)
    below = jnp.where(col_ids < row_ids, block, jnp.zeros_like(block))
    return jnp.where(col_ids == row_ids, jnp.ones_like(block), below)


def body(
    leaf_rhs,
    leaf_inverse,
    leaf_couple,
    couple_mask,
    leaf_diag,
    sep_rhs,
    sep_inverse,
    sep_couple,
    sep_diag,
):
    levels = leaf_couple.shape[1]
    layers = lax.axis_size("layer")
    own_rows = sep_rhs.shape[1]
    layer_id = lax.axis_index("layer")
    plane_id = lax.axis_index("plane")
    first_row = plane_id * own_rows
    leaf_lower = lower_unit(leaf_inverse, 0)
    leaf_y = jnp.einsum(
        "bij,bjr->bir", leaf_lower, leaf_rhs, preferred_element_type=jnp.float32
    ).astype(jnp.bfloat16)
    masked = leaf_couple * couple_mask.astype(jnp.bfloat16)[:, :, None, None]
    totals = lax.psum_scatter(
        jnp.einsum("bksc,bcr->skr", masked, leaf_y, preferred_element_type=jnp.float32),
        "plane",
        scatter_dimension=0,
        tiled=True,
    )
    sep_ids = [
        layers - (layers >> level - 1) + jnp.right_shift(layer_id, level)
        for level in range(1, levels + 1)
    ]

    def select_sep(array, level):
        return lax.dynamic_index_in_dim(array, sep_ids[level - 1], 0, keepdims=False)

    inverses = [
        lower_unit(select_sep(sep_inverse, level), first_row) for level in range(1, levels + 1)
    ]
    sep_z = []
    for level in range(1, levels + 1):
        partner = from_partner(totals[:, level - 1 :], "layer", level - 1)
        totals = jnp.concatenate([totals[:, : level - 1], totals[:, level - 1 :] + partner], axis=1)
        residual = (select_sep(sep_rhs, level).astype(jnp.float32) - totals[:, level - 1]).astype(
            jnp.bfloat16
        )
        residual_full = lax.all_gather(residual, "plane", axis=0, tiled=True)
        solved = jnp.dot(
            inverses[level - 1], residual_full, preferred_element_type=jnp.float32
        ).astype(jnp.bfloat16)
        if level < levels:
            solved_full = lax.all_gather(solved, "plane", axis=0, tiled=True)
        if level < levels:
            blocks = select_sep(sep_couple, level)[: levels - level]
            coupling = jnp.einsum(
                "jos,sr->ojr", blocks, solved_full, preferred_element_type=jnp.float32
            )
            totals = jnp.concatenate([totals[:, :level], totals[:, level:] + coupling], axis=1)
        sep_z.append(solved.astype(jnp.float32) / select_sep(sep_diag, level)[:, None])
    answers = [None] * levels
    for level in range(levels, 0, -1):
        if level < levels:
            blocks = select_sep(sep_couple, level)[: levels - level]
            upper_rows = jnp.stack(answers[level:])

            def couple_back(offset_row, row_count, blocks=blocks, upper_rows=upper_rows):
                return jnp.einsum(
                    "jos,jor->sr", blocks, upper_rows, preferred_element_type=jnp.float32
                )

            carried = lax.psum_scatter(
                couple_back(jnp.int32(0), lax.axis_size("plane") * own_rows),
                "plane",
                scatter_dimension=0,
                tiled=True,
            )
            target_now = (sep_z[level - 1] - carried).astype(jnp.bfloat16)
        else:
            target_now = sep_z[level - 1].astype(jnp.bfloat16)
        lower_part = inverses[level - 1]

        def transpose_solve(offset_row, row_count, lower_part=lower_part, target_now=target_now):
            return lax.dot_general(
                lower_part, target_now, (((0,), (0,)), ((), ())), preferred_element_type=jnp.float32
            )

        answers[level - 1] = lax.psum_scatter(
            transpose_solve(jnp.int32(0), lax.axis_size("plane") * own_rows),
            "plane",
            scatter_dimension=0,
            tiled=True,
        ).astype(jnp.bfloat16)
    above = lax.all_gather(jnp.stack(answers), "plane", axis=1, tiled=True)
    back_terms = jnp.einsum("bksc,ksr->bcr", masked, above, preferred_element_type=jnp.float32)
    leaf_target = (leaf_y.astype(jnp.float32) / leaf_diag[:, :, None] - back_terms).astype(
        jnp.bfloat16
    )
    leaf_solution = jnp.einsum(
        "bjc,bjr->bcr", leaf_lower, leaf_target, preferred_element_type=jnp.float32
    ).astype(jnp.bfloat16)
    sep_solution = jnp.stack(answers)[None]
    return (leaf_solution, sep_solution)


def solution(mesh):
    in_specs = (
        P(("layer", "plane"), None, None),
        P(("layer", "plane"), None, None),
        P(("layer", "plane"), None, None, None),
        P(("layer", "plane"), None),
        P(("layer", "plane"), None),
        P(None, "plane", None),
        P(None, "plane", None),
        P(None, None, "plane", None),
        P(None, "plane"),
    )
    out_specs = (P(("layer", "plane"), None, None), P("layer", None, "plane", None))
    return jax.shard_map(body, mesh=mesh, in_specs=in_specs, out_specs=out_specs, check_vma=False)
```

profile of v0, /device:TPU:1, one launch (start us, length us, event | category | flops | bytes accessed | tf_op | source)
XLA Modules:
  0.0 960.2 jit_solution(12969961117015314941)
XLA Ops:
  7.2 0.0 all-reduce.3.cloned.1.call-start
  7.3 0.8 convert_element_type.80
  8.0 0.1 copy.20
  8.1 0.3 copy-done
  8.4 1.4 convolution_convert_fusion
  9.8 8.7 fusion.7
  18.5 9.5 copy.23
  27.9 0.0 all-reduce.3.cloned.1.call-update
  28.0 0.0 all-gather.7.cloned.1.call-start
  28.0 0.6 copy-done.7
  28.6 0.6 dynamic-slice
  29.8 132.8 %all-reduce.3.cloned.1.call-done = f32[1024,3,512]{2,1,0:T(4,128)} async-done(((f32[1024,3,512]{2,1,0:T(4,128)}), f32[1024,3,512]{2,1,0:T(4,128)}) %all-reduce.3.cloned.1.call-update) | async-done | bytes 6291472
  162.6 1.0 constant_dynamic-slice_fusion.3
  163.6 0.1 copy.25
  163.7 1.4 collective-permute-start
  165.1 4.3 collective-permute-done
  169.3 0.1 copy_add_fusion
  169.4 1.4 fusion.57
  170.8 0.0 all-gather.7.cloned.1.call-update
  170.8 0.0 all-gather.9.cloned.1.call-start
  170.9 49.2 %all-gather.7.cloned.1.call-done = bf16[1024,512]{1,0:T(8,128)(2,1)} async-done(((bf16[32,512]{1,0:T(8,128)(2,1)}), bf16[1024,512]{1,0:T(8,128)(2,1)}) %all-gather.7.cloned.1.call-update) | async-done | bytes 1048592 | tf_op jit(solution)/shard_map/all_gather | solution.py:68
  220.1 2.2 convolution_convert_fusion.3
  222.2 0.0 all-gather.9.cloned.1.call-update
  222.2 0.0 all-gather.11.cloned.1.call-start
  222.3 48.4 %all-gather.9.cloned.1.call-done = bf16[1024,512]{1,0:T(8,128)(2,1)} async-done(((bf16[32,512]{1,0:T(8,128)(2,1)}), bf16[1024,512]{1,0:T(8,128)(2,1)}) %all-gather.9.cloned.1.call-update) | async-done | bytes 1048592 | tf_op jit(solution)/shard_map/all_gather | solution.py:73
  270.7 1.5 slice_add_fusion
  272.3 2.3 collective-permute-start.1
  274.6 6.3 collective-permute-done.1
  280.9 1.4 fusion.55
  282.3 0.0 all-gather.11.cloned.1.call-update
  282.4 0.0 all-gather.13.cloned.1.call-start
  282.4 48.1 %all-gather.11.cloned.1.call-done = bf16[1024,512]{1,0:T(8,128)(2,1)} async-done(((bf16[32,512]{1,0:T(8,128)(2,1)}), bf16[1024,512]{1,0:T(8,128)(2,1)}) %all-gather.11.cloned.1.call-update) | async-done | bytes 1048592 | tf_op jit(solution)/shard_map/all_gather | solution.py:68
  330.5 2.2 convolution_convert_fusion.2
  332.7 0.0 all-gather.13.cloned.1.call-update
  332.7 0.0 all-gather.15.cloned.1.call-start
  332.7 48.3 %all-gather.13.cloned.1.call-done = bf16[1024,512]{1,0:T(8,128)(2,1)} async-done(((bf16[32,512]{1,0:T(8,128)(2,1)}), bf16[1024,512]{1,0:T(8,128)(2,1)}) %all-gather.13.cloned.1.call-update) | async-done | bytes 1048592 | tf_op jit(solution)/shard_map/all_gather | solution.py:73
  381.0 1.5 slice_add_fusion.1
  382.5 5.5 collective-permute-start.2
  388.0 2.1 collective-permute-done.2
  390.1 1.4 fusion.61
  391.5 0.0 all-gather.15.cloned.1.call-update
  391.6 0.0 reduce-scatter.6.cloned.1.call-start
  391.6 0.8 fusion.85
  392.4 48.5 %all-gather.15.cloned.1.call-done = bf16[1024,512]{1,0:T(8,128)(2,1)} async-done(((bf16[32,512]{1,0:T(8,128)(2,1)}), bf16[1024,512]{1,0:T(8,128)(2,1)}) %all-gather.15.cloned.1.call-update) | async-done | bytes 1048592 | tf_op jit(solution)/shard_map/all_gather | solution.py:68
  440.9 3.3 fusion.28
  444.2 0.0 reduce-scatter.8.cloned.1.call-start
  444.3 84.7 %reduce-scatter.6.cloned.1.call-done = f32[32,512]{1,0:T(8,128)} async-done(((f32[1024,512]{1,0:T(8,128)}), f32[32,512]{1,0:T(8,128)}) %reduce-scatter.6.cloned.1.call-update) | async-done | bytes 65552 | tf_op jit(solution)/shard_map/reduce_scatter | solution.py:108
  529.0 2.7 fusion.68
  531.7 0.0 reduce-scatter.10.cloned.1.call-start
  531.8 87.4 %reduce-scatter.8.cloned.1.call-done = f32[32,512]{1,0:T(8,128)} async-done(((f32[1024,512]{1,0:T(8,128)}), f32[32,512]{1,0:T(8,128)}) %reduce-scatter.8.cloned.1.call-update) | async-done | bytes 65552 | tf_op jit(solution)/shard_map/reduce_scatter | solution.py:92
  619.2 2.7 fusion.69
  622.0 0.0 reduce-scatter.12.cloned.1.call-start
  622.0 87.4 %reduce-scatter.10.cloned.1.call-done = f32[32,512]{1,0:T(8,128)} async-done(((f32[1024,512]{1,0:T(8,128)}), f32[32,512]{1,0:T(8,128)}) %reduce-scatter.10.cloned.1.call-update) | async-done | bytes 65552 | tf_op jit(solution)/shard_map/reduce_scatter | solution.py:108
  709.5 0.8 convert_bitcast_fusion.1
  710.3 2.7 convolution_bitcast_fusion
  713.1 0.0 reduce-scatter.14.cloned.1.call-start
  713.1 86.4 %reduce-scatter.12.cloned.1.call-done = f32[32,512]{1,0:T(8,128)} async-done(((f32[1024,512]{1,0:T(8,128)}), f32[32,512]{1,0:T(8,128)}) %reduce-scatter.12.cloned.1.call-update) | async-done | bytes 65552 | tf_op jit(solution)/shard_map/reduce_scatter | solution.py:92
  799.5 2.7 fusion.70
  802.3 0.0 all-gather.17.cloned.1.call-start
  802.3 87.4 %reduce-scatter.14.cloned.1.call-done = f32[32,512]{1,0:T(8,128)} async-done(((f32[1024,512]{1,0:T(8,128)}), f32[32,512]{1,0:T(8,128)}) %reduce-scatter.14.cloned.1.call-update) | async-done | bytes 65552 | tf_op jit(solution)/shard_map/reduce_scatter | solution.py:108
  889.8 0.8 convert_bitcast_fusion
  890.6 0.7 fusion.101
  891.3 53.4 %all-gather.17.cloned.1.call-done = bf16[3,1024,512]{2,1,0:T(8,128)(2,1)} async-done(((bf16[3,32,512]{2,1,0:T(8,128)(2,1)}), bf16[3,1024,512]{2,1,0:T(8,128)(2,1)}) %all-gather.17.cloned.1.call-update) | async-done | bytes 3145744 | tf_op jit(solution)/shard_map/all_gather | solution.py:114
  944.8 8.6 fusion.20
  (24 shorter events, 0.2 us)
Async XLA Ops:
  7.2 1.2 copy-start
  7.2 155.5 %all-reduce.3.cloned.1.call-start = ((), (), s32[]{:S(2)}) async-start(), calls=%async_computation.16 | async-start | bytes 16777216
  27.9 0.7 copy-start.7
  27.9 192.1 %copy-start.1 = (bf16[7,32,1024]{2,1,0:T(8,128)(2,1)S(1)}, bf16[7,32,1024]{2,1,0:T(8,128)(2,1)}, u32[]{:S(2)}) copy-start(bf16[7,32,1024]{2,1,0:T(8,128)(2,1)} %param.15) | copy-start | bytes 1376260
  28.0 192.1 %all-gather.7.cloned.1.call-start = ((), (), s32[]{:S(2)}) async-start(), calls=%async_computation.5 | async-start | bytes 1081344 | tf_op jit(solution)/shard_map/all_gather | solution.py:68
  163.7 5.6 collective-permute-start
  170.8 99.9 %all-gather.9.cloned.1.call-start = ((), (), s32[]{:S(2)}) async-start(), calls=%async_computation.6 | async-start | bytes 1081344 | tf_op jit(solution)/shard_map/all_gather | solution.py:73
  222.2 108.2 %all-gather.11.cloned.1.call-start = ((), (), s32[]{:S(2)}) async-start(), calls=%async_computation.7 | async-start | bytes 1081344 | tf_op jit(solution)/shard_map/all_gather | solution.py:68
  272.3 8.7 collective-permute-start.1
  282.4 98.7 %all-gather.13.cloned.1.call-start = ((), (), s32[]{:S(2)}) async-start(), calls=%async_computation.8 | async-start | bytes 1081344 | tf_op jit(solution)/shard_map/all_gather | solution.py:73
  332.7 108.2 %all-gather.15.cloned.1.call-start = ((), (), s32[]{:S(2)}) async-start(), calls=%async_computation.9 | async-start | bytes 1081344 | tf_op jit(solution)/shard_map/all_gather | solution.py:68
  382.5 7.6 collective-permute-start.2
  391.6 137.5 %reduce-scatter.6.cloned.1.call-start = ((), (), s32[]{:S(2)}) async-start(), calls=%async_computation.10 | async-start | bytes 2162688 | tf_op jit(solution)/shard_map/reduce_scatter | solution.py:108
  444.2 175.0 %copy-start.3 = (bf16[32,512]{1,0:T(8,128)(2,1)S(1)}, bf16[32,512]{1,0:T(8,128)(2,1)}, u32[]{:S(2)}) copy-start(bf16[32,512]{1,0:T(8,128)(2,1)} %convolution_convert_fusion.2) | copy-start | bytes 98308
  444.2 175.0 %reduce-scatter.8.cloned.1.call-start = ((), (), s32[]{:S(2)}) async-start(), calls=%async_computation.11 | async-start | bytes 2162688 | tf_op jit(solution)/shard_map/reduce_scatter | solution.py:92
  531.7 90.3 %copy-start.5 = (f32[32,512]{1,0:T(8,128)S(1)}, f32[32,512]{1,0:T(8,128)}, u32[]{:S(2)}) copy-start(f32[32,512]{1,0:T(8,128)} %reduce-scatter.6.cloned.1.call-done) | copy-start | bytes 196612
  531.7 177.7 %reduce-scatter.10.cloned.1.call-start = ((), (), s32[]{:S(2)}) async-start(), calls=%async_computation.12 | async-start | bytes 2162688 | tf_op jit(solution)/shard_map/reduce_scatter | solution.py:108
  621.9 177.6 %copy-start.2 = (bf16[32,512]{1,0:T(8,128)(2,1)S(1)}, bf16[32,512]{1,0:T(8,128)(2,1)}, u32[]{:S(2)}) copy-start(bf16[32,512]{1,0:T(8,128)(2,1)} %convolution_convert_fusion.3) | copy-start | bytes 98308
  622.0 177.6 %reduce-scatter.12.cloned.1.call-start = ((), (), s32[]{:S(2)}) async-start(), calls=%async_computation.13 | async-start | bytes 2162688 | tf_op jit(solution)/shard_map/reduce_scatter | solution.py:92
  713.0 231.7 %copy-start.4 = (bf16[8,128,128]{2,1,0:T(8,128)(2,1)S(1)}, bf16[8,128,128]{2,1,0:T(8,128)(2,1)}, u32[]{:S(2)}) copy-start(bf16[8,128,128]{2,1,0:T(8,128)(2,1)} %param.10) | copy-start | bytes 786436
  713.0 231.7 %copy-start.6 = (f32[8,128]{1,0:T(8,128)S(1)}, f32[8,128]{1,0:T(8,128)}, u32[]{:S(2)}) copy-start(f32[8,128]{1,0:T(8,128)} %param.13) | copy-start | bytes 12292
  713.1 176.7 %reduce-scatter.14.cloned.1.call-start = ((), (), s32[]{:S(2)}) async-start(), calls=%async_computation.14 | async-start | bytes 2162688 | tf_op jit(solution)/shard_map/reduce_scatter | solution.py:108
  802.3 142.5 %all-gather.17.cloned.1.call-start = ((), (), s32[]{:S(2)}) async-start(), calls=%async_computation.15 | async-start | bytes 3244032 | tf_op jit(solution)/shard_map/all_gather | solution.py:114
Sparse Core Ops, SparseCore 0:
  28.1 134.5 all-reduce.2
  171.0 49.0 all-gather.6
  223.5 47.1 all-gather.8
  282.5 47.9 all-gather.10
  333.8 47.1 all-gather.12
  391.7 49.1 all-gather.14
  445.2 83.7 reduce-scatter.5
  533.3 85.8 reduce-scatter.7
  623.5 85.8 reduce-scatter.9
  713.6 85.8 reduce-scatter.11
  803.9 85.8 reduce-scatter.13
  893.1 51.5 all-gather.16
where the time goes:
time: 961 us; the launch traced here: 960 us
  waiting for transfers between devices  875 us (91%)
  matrix products  40.2 us (4%)
  between operations  15 us (2%)
  local copies, waits for them, and re-layouts  12.9 us (1%)
  starting transfers between devices  9.71 us (1%)
    reduce_scatter x3, waiting for transfers between devices, body(): lax.psum_scatter(transpose_solve(jnp.int32(0), lax.axis_size('plane') * o...  260 us
    reduce_scatter x2, waiting for transfers between devices, body(): lax.psum_scatter(couple_back(jnp.int32(0), lax.axis_size('plane') * own_r...  174 us
    all_gather x3, waiting for transfers between devices, body(): residual_full = lax.all_gather(residual, 'plane', axis=0, tiled=True)  146 us
    unnamed x13, waiting for transfers between devices  133 us
    all_gather x2, waiting for transfers between devices, body(): solved_full = lax.all_gather(solved, 'plane', axis=0, tiled=True)  96.7 us
    all_gather x1, waiting for transfers between devices, body(): above = lax.all_gather(jnp.stack(answers), 'plane', axis=1, tiled=True)  53.4 us
  transfers between devices with their start and end apart: 15, of which 15 were waited for; matrix products, arithmetic and copies ran while one was open for 0% of the time, Pallas kernels for 0%

commit v1 on v0

--- a/solution.py
+++ b/solution.py
@@ -111,7 +111,10 @@
             scatter_dimension=0,
             tiled=True,
         ).astype(jnp.bfloat16)
-    above = lax.all_gather(jnp.stack(answers), "plane", axis=1, tiled=True)
+    above = jnp.concatenate(
+        lax.all_to_all(jnp.stack([jnp.stack(answers)] * lax.axis_size("plane")), "plane", 0, 0),
+        axis=1,
+    )
     back_terms = jnp.einsum("bksc,ksr->bcr", masked, above, preferred_element_type=jnp.float32)
     leaf_target = (leaf_y.astype(jnp.float32) / leaf_diag[:, :, None] - back_terms).astype(
         jnp.bfloat16

time: 961 us -> 957 us (level)
  waiting for transfers between devices: 875 us -> 822 us
  blocking collectives: 0 us -> 46.8 us
    all_gather x1 -> x0, waiting for transfers between devices: 53.4 us -> none  [body(): above = lax.all_gather(jnp.stack(answers), 'plane', axis=1, tiled=True)]
    all_to_all x0 -> x1, blocking collectives: none -> 46.8 us  [body(): lax.all_to_all(jnp.stack([jnp.stack(answers)] * lax.axis_size('plane')),...]
    unnamed x13 -> x12, waiting for transfers between devices: 133 us -> 133 us
  transfers between devices with their start and end apart: 15 -> 14, of which waited for: 15 -> 14; matrix products, arithmetic and copies ran while one was open for 0% -> 0% of each run, Pallas kernels for 0% -> 0%
where the time goes in v1:
time: 957 us; the launch traced here: 956 us
  waiting for transfers between devices  822 us (86%)
  blocking collectives  46.8 us (5%)
  matrix products  40.1 us (4%)
  local copies, waits for them, and re-layouts  15.4 us (2%)
  between operations  14.6 us (2%)
  starting transfers between devices  9.67 us (1%)
    reduce_scatter x3, waiting for transfers between devices, body(): lax.psum_scatter(transpose_solve(jnp.int32(0), lax.axis_size('plane') * o...  260 us
    reduce_scatter x2, waiting for transfers between devices, body(): lax.psum_scatter(couple_back(jnp.int32(0), lax.axis_size('plane') * own_r...  174 us
    all_gather x3, waiting for transfers between devices, body(): residual_full = lax.all_gather(residual, 'plane', axis=0, tiled=True)  146 us
    unnamed x12, waiting for transfers between devices  133 us
    all_gather x2, waiting for transfers between devices, body(): solved_full = lax.all_gather(solved, 'plane', axis=0, tiled=True)  96.7 us
    all_to_all x1, blocking collectives, body(): lax.all_to_all(jnp.stack([jnp.stack(answers)] * lax.axis_size('plane')),...  46.8 us
  transfers between devices with their start and end apart: 14, of which 14 were waited for; matrix products, arithmetic and copies ran while one was open for 0% of the time, Pallas kernels for 0%

profile of v1, /device:TPU:1, one launch (start us, length us, event | category | flops | bytes accessed | tf_op | source)
XLA Modules:
  0.0 955.6 jit_solution(9984068140575591758)
XLA Ops:
  7.2 0.0 all-reduce.3.cloned.1.call-start
  7.3 0.8 convert_element_type.80
  8.0 0.1 copy.29
  8.1 0.3 copy-done
  8.4 1.4 convolution_convert_fusion
  9.8 8.7 fusion.6
  18.4 9.5 copy.32
  27.9 0.0 all-gather.6.cloned.1.call-start
  28.0 0.6 copy-done.7
  28.6 0.6 dynamic-slice
  29.8 132.8 %all-reduce.3.cloned.1.call-done = f32[1024,3,512]{2,1,0:T(4,128)} async-done(((f32[1024,3,512]{2,1,0:T(4,128)}), f32[1024,3,512]{2,1,0:T(4,128)}) %all-reduce.3.cloned.1.call-update) | async-done | bytes 6291472
  162.6 1.0 constant_dynamic-slice_fusion.3
  163.6 0.1 copy.34
  163.7 1.4 collective-permute-start
  165.1 4.3 collective-permute-done
  169.3 0.1 copy_add_fusion
  169.4 1.4 fusion.50
  170.8 0.0 all-gather.6.cloned.1.call-update
  170.8 0.0 all-gather.8.cloned.1.call-start
  170.9 49.2 %all-gather.6.cloned.1.call-done = bf16[1024,512]{1,0:T(8,128)(2,1)} async-done(((bf16[32,512]{1,0:T(8,128)(2,1)}), bf16[1024,512]{1,0:T(8,128)(2,1)}) %all-gather.6.cloned.1.call-update) | async-done | bytes 1048592 | tf_op jit(solution)/shard_map/all_gather | solution.py:68
  220.0 2.2 convolution_convert_fusion.3
  222.2 0.0 all-gather.10.cloned.1.call-start
  222.3 48.4 %all-gather.8.cloned.1.call-done = bf16[1024,512]{1,0:T(8,128)(2,1)} async-done(((bf16[32,512]{1,0:T(8,128)(2,1)}), bf16[1024,512]{1,0:T(8,128)(2,1)}) %all-gather.8.cloned.1.call-update) | async-done | bytes 1048592 | tf_op jit(solution)/shard_map/all_gather | solution.py:73
  270.7 1.5 slice_add_fusion
  272.2 2.4 collective-permute-start.1
  274.6 6.3 collective-permute-done.1
  280.9 1.4 fusion.48
  282.3 0.0 all-gather.10.cloned.1.call-update
  282.3 0.0 all-gather.12.cloned.1.call-start
  282.4 48.1 %all-gather.10.cloned.1.call-done = bf16[1024,512]{1,0:T(8,128)(2,1)} async-done(((bf16[32,512]{1,0:T(8,128)(2,1)}), bf16[1024,512]{1,0:T(8,128)(2,1)}) %all-gather.10.cloned.1.call-update) | async-done | bytes 1048592 | tf_op jit(solution)/shard_map/all_gather | solution.py:68
  330.5 2.2 convolution_convert_fusion.2
  332.6 0.0 all-gather.12.cloned.1.call-update
  332.7 0.0 all-gather.14.cloned.1.call-start
  332.7 48.3 %all-gather.12.cloned.1.call-done = bf16[1024,512]{1,0:T(8,128)(2,1)} async-done(((bf16[32,512]{1,0:T(8,128)(2,1)}), bf16[1024,512]{1,0:T(8,128)(2,1)}) %all-gather.12.cloned.1.call-update) | async-done | bytes 1048592 | tf_op jit(solution)/shard_map/all_gather | solution.py:73
  381.0 1.5 slice_add_fusion.1
  382.5 5.5 collective-permute-start.2
  388.0 2.1 collective-permute-done.2
  390.1 1.4 fusion.54
  391.5 0.0 all-gather.14.cloned.1.call-update
  391.5 0.0 reduce-scatter.6.cloned.1.call-start
  391.6 0.8 fusion.78
  392.4 48.5 %all-gather.14.cloned.1.call-done = bf16[1024,512]{1,0:T(8,128)(2,1)} async-done(((bf16[32,512]{1,0:T(8,128)(2,1)}), bf16[1024,512]{1,0:T(8,128)(2,1)}) %all-gather.14.cloned.1.call-update) | async-done | bytes 1048592 | tf_op jit(solution)/shard_map/all_gather | solution.py:68
  440.9 3.3 fusion.21
  444.2 0.0 reduce-scatter.8.cloned.1.call-start
  444.2 84.8 %reduce-scatter.6.cloned.1.call-done = f32[32,512]{1,0:T(8,128)} async-done(((f32[1024,512]{1,0:T(8,128)}), f32[32,512]{1,0:T(8,128)}) %reduce-scatter.6.cloned.1.call-update) | async-done | bytes 65552 | tf_op jit(solution)/shard_map/reduce_scatter | solution.py:108
  529.0 2.7 fusion.61
  531.7 0.0 reduce-scatter.8.cloned.1.call-update
  531.7 0.0 reduce-scatter.10.cloned.1.call-start
  531.7 87.5 %reduce-scatter.8.cloned.1.call-done = f32[32,512]{1,0:T(8,128)} async-done(((f32[1024,512]{1,0:T(8,128)}), f32[32,512]{1,0:T(8,128)}) %reduce-scatter.8.cloned.1.call-update) | async-done | bytes 65552 | tf_op jit(solution)/shard_map/reduce_scatter | solution.py:92
  619.2 2.7 fusion.62
  621.9 0.0 reduce-scatter.12.cloned.1.call-start
  622.0 87.4 %reduce-scatter.10.cloned.1.call-done = f32[32,512]{1,0:T(8,128)} async-done(((f32[1024,512]{1,0:T(8,128)}), f32[32,512]{1,0:T(8,128)}) %reduce-scatter.10.cloned.1.call-update) | async-done | bytes 65552 | tf_op jit(solution)/shard_map/reduce_scatter | solution.py:108
  709.4 0.8 convert_bitcast_fusion.1
  710.3 2.7 convolution_bitcast_fusion
  713.0 0.0 reduce-scatter.14.cloned.1.call-start
  713.1 86.5 %reduce-scatter.12.cloned.1.call-done = f32[32,512]{1,0:T(8,128)} async-done(((f32[1024,512]{1,0:T(8,128)}), f32[32,512]{1,0:T(8,128)}) %reduce-scatter.12.cloned.1.call-update) | async-done | bytes 65552 | tf_op jit(solution)/shard_map/reduce_scatter | solution.py:92
  799.5 2.7 fusion.63
  802.2 87.5 %reduce-scatter.14.cloned.1.call-done = f32[32,512]{1,0:T(8,128)} async-done(((f32[1024,512]{1,0:T(8,128)}), f32[32,512]{1,0:T(8,128)}) %reduce-scatter.14.cloned.1.call-update) | async-done | bytes 65552 | tf_op jit(solution)/shard_map/reduce_scatter | solution.py:108
  889.7 0.8 convert_bitcast_fusion
  890.6 0.7 fusion.94
  891.3 0.4 stack.19
  891.6 46.8 %all_to_all.5 = bf16[32,3,32,512]{3,2,1,0:T(8,128)(2,1)S(1)} all-to-all(bf16[32,3,32,512]{3,2,1,0:T(8,128)(2,1)S(1)} %stack.19), channel_id=1, replica_groups=mesh['layer'=8,'plane'=32] {'plane'}, dimensions={0} | all-to-all | bytes 6291456 | tf_op jit(solution)/shard_map/all_to_all | solution.py:115
  938.4 2.0 copy.35
  940.5 8.6 fusion.15
  (24 shorter events, 0.2 us)
Async XLA Ops:
  7.2 1.2 copy-start
  7.2 155.4 %all-reduce.3.cloned.1.call-start = ((), (), s32[]{:S(2)}) async-start(), calls=%async_computation.16 | async-start | bytes 16777216
  27.9 0.7 copy-start.7
  27.9 192.1 %copy-start.1 = (bf16[7,32,1024]{2,1,0:T(8,128)(2,1)S(1)}, bf16[7,32,1024]{2,1,0:T(8,128)(2,1)}, u32[]{:S(2)}) copy-start(bf16[7,32,1024]{2,1,0:T(8,128)(2,1)} %param.15) | copy-start | bytes 1376260
  27.9 192.1 %all-gather.6.cloned.1.call-start = ((), (), s32[]{:S(2)}) async-start(), calls=%async_computation.6 | async-start | bytes 1081344 | tf_op jit(solution)/shard_map/all_gather | solution.py:68
  163.7 5.6 collective-permute-start
  170.8 99.9 %all-gather.8.cloned.1.call-start = ((), (), s32[]{:S(2)}) async-start(), calls=%async_computation.7 | async-start | bytes 1081344 | tf_op jit(solution)/shard_map/all_gather | solution.py:73
  222.2 108.2 %all-gather.10.cloned.1.call-start = ((), (), s32[]{:S(2)}) async-start(), calls=%async_computation.8 | async-start | bytes 1081344 | tf_op jit(solution)/shard_map/all_gather | solution.py:68
  272.2 8.7 collective-permute-start.1
  282.3 98.7 %all-gather.12.cloned.1.call-start = ((), (), s32[]{:S(2)}) async-start(), calls=%async_computation.9 | async-start | bytes 1081344 | tf_op jit(solution)/shard_map/all_gather | solution.py:73
  332.7 108.2 %all-gather.14.cloned.1.call-start = ((), (), s32[]{:S(2)}) async-start(), calls=%async_computation.10 | async-start | bytes 1081344 | tf_op jit(solution)/shard_map/all_gather | solution.py:68
  382.5 7.6 collective-permute-start.2
  391.5 137.5 %reduce-scatter.6.cloned.1.call-start = ((), (), s32[]{:S(2)}) async-start(), calls=%async_computation.11 | async-start | bytes 2162688 | tf_op jit(solution)/shard_map/reduce_scatter | solution.py:108
  444.2 175.0 %copy-start.3 = (bf16[32,512]{1,0:T(8,128)(2,1)S(1)}, bf16[32,512]{1,0:T(8,128)(2,1)}, u32[]{:S(2)}) copy-start(bf16[32,512]{1,0:T(8,128)(2,1)} %convolution_convert_fusion.2) | copy-start | bytes 98308
  444.2 175.0 %reduce-scatter.8.cloned.1.call-start = ((), (), s32[]{:S(2)}) async-start(), calls=%async_computation.12 | async-start | bytes 2162688 | tf_op jit(solution)/shard_map/reduce_scatter | solution.py:92
  531.7 90.3 %copy-start.5 = (f32[32,512]{1,0:T(8,128)S(1)}, f32[32,512]{1,0:T(8,128)}, u32[]{:S(2)}) copy-start(f32[32,512]{1,0:T(8,128)} %reduce-scatter.6.cloned.1.call-done) | copy-start | bytes 196612
  531.7 177.7 %reduce-scatter.10.cloned.1.call-start = ((), (), s32[]{:S(2)}) async-start(), calls=%async_computation.13 | async-start | bytes 2162688 | tf_op jit(solution)/shard_map/reduce_scatter | solution.py:108
  621.9 177.6 %copy-start.2 = (bf16[32,512]{1,0:T(8,128)(2,1)S(1)}, bf16[32,512]{1,0:T(8,128)(2,1)}, u32[]{:S(2)}) copy-start(bf16[32,512]{1,0:T(8,128)(2,1)} %convolution_convert_fusion.3) | copy-start | bytes 98308
  621.9 177.6 %reduce-scatter.12.cloned.1.call-start = ((), (), s32[]{:S(2)}) async-start(), calls=%async_computation.14 | async-start | bytes 2162688 | tf_op jit(solution)/shard_map/reduce_scatter | solution.py:92
  713.0 176.7 %reduce-scatter.14.cloned.1.call-start = ((), (), s32[]{:S(2)}) async-start(), calls=%async_computation.15 | async-start | bytes 2162688 | tf_op jit(solution)/shard_map/reduce_scatter | solution.py:108
  938.4 2.1 copy-start.4
  938.4 2.1 copy-start.6
Sparse Core Ops, SparseCore 0:
  28.1 134.5 all-reduce.2
  170.9 49.0 all-gather.5
  223.5 47.1 all-gather.7
  282.5 47.9 all-gather.9
  333.8 47.1 all-gather.11
  391.7 49.1 all-gather.13
  445.2 83.7 reduce-scatter.5
  533.3 85.8 reduce-scatter.7
  623.5 85.8 reduce-scatter.9
  713.6 85.8 reduce-scatter.11
  803.8 85.8 reduce-scatter.13
